TPU v7x, 32 devices: a whole 2x2x4 slice. The times are simulated.
32 devices in a mesh: seq: 8 (over z, x), head: 4 (over y, core).
Axes of the slice: x: 2, y: 2, z: 4, core: 2. Of those that a mesh axis runs over, the one named last changes fastest.
Arguments:
- queries: bfloat16 [4, 64, 64, 128], P(None, 'seq', 'head')
- new_kv: bfloat16 [2, 4, 64, 8, 128], P(None, None, 'seq', 'head'), may hold values from -12 to 12
- prompt_keys: bfloat16 [8, 8192, 8, 128], P(None, 'seq', 'head')
- prompt_values: bfloat16 [8, 8192, 8, 128], P(None, 'seq', 'head'), may hold values from -6 to 6
- suffix_kv: bfloat16 [2, 64, 512, 8, 128], P(None, 'seq', None, 'head'), may hold values from -9.5625 to 9.5625
- prompt_ids: int32 [64, 1], P('seq'), may hold values from 0 to 7
- suffix_lengths: int32 [64], P('seq'), may hold values from 1 to 512, 16384 in all
- token_ids: int32 [64, 4], replicated, may hold values from 0 to 65535
- embedding: bfloat16 [65536, 8192], P('head', 'seq'), may hold values from -3 to 3
- out_weight: bfloat16 [8192, 8192], P('head', 'seq'), may hold values from -0.25 to 0.25
Outputs:
- hidden_out: bfloat16 [64, 4, 8192], P('head', None, 'seq')
Inputs may be any that keep to these rules, and one draw needn't show every extreme that they name: `prompt_ids`: every one of the 8 prompts is named by some row.
All inputs are finite; a program needn't handle non-finite values. No bound on the sum of `suffix_lengths` on one device may be relied on, other than what follows from the above.
Results may differ from a plain program's by a relative error of at most 0.02.
Values may be sent and summed in bfloat16 or wider, within the bound.
A program may use at most 320 MiB of HBM per device.

v0:
```python
import math

import jax
import jax.numpy as jnp
from jax import lax
from jax.sharding import PartitionSpec as P


def shards(
    queries,
    new_kv,
    prompt_keys,
    prompt_values,
    suffix_kv,
    prompt_ids,
    suffix_lengths,
    token_ids,
    embedding,
    out_weight,
):
    step_count, rows_own, heads_own, head_dim = queries.shape
    kv_own = prompt_keys.shape[2]
    group_size = heads_own // kv_own
    score_scale = head_dim ** (-0.5)
    prompt_total = prompt_keys.shape[0]
    gathered_q, gathered_ids = (
        lax.all_gather(queries, "seq", axis=1, tiled=True),
        lax.all_gather(prompt_ids.reshape(1, rows_own), "seq", axis=1, tiled=True),
    )
    all_rows = gathered_q.shape[1]
    block_rows = math.gcd(all_rows, 32)
    row_ids = gathered_ids[0].astype(jnp.int32)
    order = jnp.argsort(row_ids, stable=True)
    inverse = jnp.argsort(order, stable=True)
    counts = jnp.sum(
        (row_ids[:, None] == jnp.arange(prompt_total, dtype=jnp.int32)[None, :]).astype(jnp.int32),
        axis=0,
    )
    starts = jnp.cumsum(counts) - counts
    sorted_q = jnp.take(gathered_q, order, axis=1)
    padding = jnp.zeros((step_count, block_rows, heads_own, head_dim), sorted_q.dtype)
    sorted_q = jnp.concatenate([sorted_q, padding], axis=1).reshape(
        step_count, all_rows + block_rows, kv_own, group_size, head_dim
    )
    padded_rows = all_rows + block_rows
    init_peak = jnp.zeros((padded_rows, kv_own, step_count, group_size), jnp.float32)
    init_mixed = jnp.zeros((padded_rows, kv_own, step_count, group_size, head_dim), jnp.float32)

    def per_prompt(prompt_index, carry):
        key_rows = lax.dynamic_index_in_dim(prompt_keys, prompt_index, 0, keepdims=False)
        value_rows = lax.dynamic_index_in_dim(prompt_values, prompt_index, 0, keepdims=False)
        first = starts[prompt_index]
        limit = first + counts[prompt_index]
        tiles = (counts[prompt_index] + block_rows - 1) // block_rows

        def per_tile(tile_index, inner):
            peak_acc, total_acc, mixed_acc = inner
            begin = first + tile_index * block_rows
            query_block = lax.dynamic_slice_in_dim(sorted_q, begin, block_rows, 1)
            scores = (
                jnp.einsum(
                    "trcgd,kcd->rctgk", query_block, key_rows, preferred_element_type=jnp.float32
                )
                * score_scale
            )
            peak = jnp.max(scores, axis=-1)
            weights = jnp.exp(scores - peak[..., None])
            total = jnp.sum(weights, axis=-1)
            mixed = jnp.einsum(
                "rctgk,kcd->rctgd",
                weights.astype(jnp.bfloat16),
                value_rows,
                preferred_element_type=jnp.float32,
            )
            valid = begin + jnp.arange(block_rows, dtype=jnp.int32) < limit
            old_peak = lax.dynamic_slice_in_dim(peak_acc, begin, block_rows, 0)
            old_total = lax.dynamic_slice_in_dim(total_acc, begin, block_rows, 0)
            old_mixed = lax.dynamic_slice_in_dim(mixed_acc, begin, block_rows, 0)
            flag = valid[:, None, None, None]
            peak_acc = lax.dynamic_update_slice_in_dim(
                peak_acc, jnp.where(flag, peak, old_peak), begin, 0
            )
            total_acc = lax.dynamic_update_slice_in_dim(
                total_acc, jnp.where(flag, total, old_total), begin, 0
            )
            mixed_acc = lax.dynamic_update_slice_in_dim(
                mixed_acc, jnp.where(flag[..., None], mixed, old_mixed), begin, 0
            )
            return (peak_acc, total_acc, mixed_acc)

        return lax.fori_loop(0, tiles, per_tile, carry)

    peak_sorted, total_sorted, mixed_sorted = lax.fori_loop(
        0, prompt_total, per_prompt, (init_peak, init_peak, init_mixed)
    )
    highest = jnp.take(peak_sorted[:all_rows], inverse, axis=0)
    summed = jnp.take(total_sorted[:all_rows], inverse, axis=0)
    blended = jnp.take(mixed_sorted[:all_rows], inverse, axis=0)
    first_row = lax.axis_index("seq") * rows_own
    global_peak = lax.pmax(highest.astype(jnp.bfloat16), "seq").astype(highest.dtype)
    factor = jnp.exp(highest - global_peak)
    own_total, own_mixed = (
        lax.psum_scatter(
            (summed * factor).astype(jnp.bfloat16), "seq", scatter_dimension=0, tiled=True
        ).astype(jnp.float32),
        lax.psum_scatter(
            (blended * factor[..., None]).astype(jnp.bfloat16),
            "seq",
            scatter_dimension=0,
            tiled=True,
        ).astype(jnp.float32),
    )
    own_peak = lax.dynamic_slice_in_dim(global_peak, first_row, rows_own, 0)
    own_q = queries.reshape(step_count, rows_own, kv_own, group_size, head_dim)
    suffix_len = suffix_kv.shape[2]
    score_suffix = (
        jnp.einsum("trcgd,rkcd->rctgk", own_q, suffix_kv[0], preferred_element_type=jnp.float32)
        * score_scale
    )
    live_mask = jnp.arange(suffix_len, dtype=jnp.int32)[None, :] < suffix_lengths[:, None]
    score_suffix = jnp.where(live_mask[:, None, None, None, :], score_suffix, -jnp.inf)
    score_fresh = (
        jnp.einsum("trcgd,urcd->rctgu", own_q, new_kv[0], preferred_element_type=jnp.float32)
        * score_scale
    )
    step_order = jnp.arange(step_count, dtype=jnp.int32)
    causal = step_order[None, :] <= step_order[:, None]
    score_fresh = jnp.where(causal[None, None, :, None, :], score_fresh, -jnp.inf)
    peak_all = jnp.maximum(
        own_peak, jnp.maximum(jnp.max(score_suffix, axis=-1), jnp.max(score_fresh, axis=-1))
    )
    carried = jnp.exp(own_peak - peak_all)
    weight_suffix = jnp.exp(score_suffix - peak_all[..., None])
    weight_fresh = jnp.exp(score_fresh - peak_all[..., None])
    denominator = (
        own_total * carried + jnp.sum(weight_suffix, axis=-1) + jnp.sum(weight_fresh, axis=-1)
    )
    numerator = own_mixed * carried[..., None]
    numerator = numerator + jnp.einsum(
        "rctgk,rkcd->rctgd",
        weight_suffix.astype(jnp.bfloat16),
        suffix_kv[1],
        preferred_element_type=jnp.float32,
    )
    numerator = numerator + jnp.einsum(
        "rctgu,urcd->rctgd",
        weight_fresh.astype(jnp.bfloat16),
        new_kv[1],
        preferred_element_type=jnp.float32,
    )
    attention = (numerator / denominator[..., None]).astype(jnp.bfloat16)
    attention_all = lax.all_gather(attention, "seq", axis=0, tiled=True)
    weight_local = out_weight.reshape(kv_own, group_size, head_dim, out_weight.shape[1])
    vocab_own = embedding.shape[0]
    vocab_first = lax.axis_index("head") * vocab_own
    projected = jnp.einsum(
        "rctgd,cgde->rte", attention_all, weight_local, preferred_element_type=jnp.float32
    )
    local_ids = token_ids - vocab_first
    inside = (local_ids >= 0) & (local_ids < vocab_own)
    embedded = jnp.take(embedding, jnp.clip(local_ids, 0, vocab_own - 1), axis=0).astype(
        jnp.float32
    )
    return lax.psum_scatter(
        (projected + jnp.where(inside[..., None], embedded, 0.0)).astype(jnp.bfloat16),
        "head",
        scatter_dimension=0,
        tiled=True,
    )


def solution(mesh):
    return jax.shard_map(
        shards,
        mesh=mesh,
        in_specs=(
            P(None, "seq", "head", None),
            P(None, None, "seq", "head", None),
            P(None, "seq", "head", None),
            P(None, "seq", "head", None),
            P(None, "seq", None, "head", None),
            P("seq", None),
            P("seq"),
            P(),
            P("head", "seq"),
            P("head", "seq"),
        ),
        out_specs=P("head", None, "seq"),
        check_vma=False,
    )
```

profile of v0, /device:TPU:21, one launch (start us, length us, event | category | flops | bytes accessed | tf_op | source)
XLA Modules:
  0.0 359.7 jit_solution(11614262959084922072)
XLA Ops:
  10.1 6.5 %all-reduce.1 = s32[64]{0:T(128)S(1)} all-reduce(s32[64]{0:T(128)S(1)} %bitcast_dynamic-update-slice_fusion), channel_id=2, replica_groups=mesh['seq'=8,'head'=4] {'seq'}, use_global_device_ids=true, to_apply=%add.1 | all-reduce | flops 64 | bytes 512 | tf_op jit(solution)/shard_map/squeeze | solution.py:32
  23.4 2.9 fusion.47
  26.3 23.5 %all-gather.4.cloned.1.call-done = bf16[4,64,16,128]{3,2,1,0:T(8,128)(2,1)} async-done(((bf16[4,8,16,128]{3,2,1,0:T(8,128)(2,1)}), bf16[4,64,16,128]{3,2,1,0:T(8,128)(2,1)}) %all-gather.4.cloned.1.call-update) | async-done | bytes 1048592 | tf_op jit(solution)/shard_map/all_gather | solution.py:27
  54.8 115.7 %while.65 = (s32[]{:T(128)}, f32[96,2,4,8]{3,0,2,1:T(8,128)S(1)}, f32[96,2,4,8]{3,0,2,1:T(8,128)S(1)}, f32[96,2,4,8,128]{4,3,2,0,1:T(8,128)}, s32[8]{0:T(128)S(1...) while((s32[]{:T(128)}, f32[96,2,4,8]{3,0,2,1:T(8,128)S(1)}, ...), condition=%wide.region_9.10_spmd, body=%wide.region_4.9_spmd.sunk | while | flops 1086586880 | bytes 58303800 | solution.py:93
  60.6 8.6 %while.66 = (s32[]{:T(128)}, f32[96,2,4,8]{3,0,2,1:T(8,128)S(1)}, f32[96,2,4,8]{3,0,2,1:T(8,128)S(1)}, f32[96,2,4,8,128]{4,3,2,0,1:T(8,128)}, s32[]{:T(128)}, /*...) while((s32[]{:T(128)}, f32[96,2,4,8]{3,0,2,1:T(8,128)S(1)}, ...), condition=%wide.region_8.8_spmd, body=%wide.region_5.7_spmd.sunk | while | flops 1086586880 | bytes 54109008 | solution.py:91
  64.6 2.4 fusion.58
  75.1 8.6 %while.66 = (s32[]{:T(128)}, f32[96,2,4,8]{3,0,2,1:T(8,128)S(1)}, f32[96,2,4,8]{3,0,2,1:T(8,128)S(1)}, f32[96,2,4,8,128]{4,3,2,0,1:T(8,128)}, s32[]{:T(128)}, /*...) while((s32[]{:T(128)}, f32[96,2,4,8]{3,0,2,1:T(8,128)S(1)}, ...), condition=%wide.region_8.8_spmd, body=%wide.region_5.7_spmd.sunk | while | flops 1086586880 | bytes 54109008 | solution.py:91
  89.5 8.6 %while.66 = (s32[]{:T(128)}, f32[96,2,4,8]{3,0,2,1:T(8,128)S(1)}, f32[96,2,4,8]{3,0,2,1:T(8,128)S(1)}, f32[96,2,4,8,128]{4,3,2,0,1:T(8,128)}, s32[]{:T(128)}, /*...) while((s32[]{:T(128)}, f32[96,2,4,8]{3,0,2,1:T(8,128)S(1)}, ...), condition=%wide.region_8.8_spmd, body=%wide.region_5.7_spmd.sunk | while | flops 1086586880 | bytes 54109008 | solution.py:91
  93.6 2.4 fusion.58
  104.0 8.6 %while.66 = (s32[]{:T(128)}, f32[96,2,4,8]{3,0,2,1:T(8,128)S(1)}, f32[96,2,4,8]{3,0,2,1:T(8,128)S(1)}, f32[96,2,4,8,128]{4,3,2,0,1:T(8,128)}, s32[]{:T(128)}, /*...) while((s32[]{:T(128)}, f32[96,2,4,8]{3,0,2,1:T(8,128)S(1)}, ...), condition=%wide.region_8.8_spmd, body=%wide.region_5.7_spmd.sunk | while | flops 1086586880 | bytes 54109008 | solution.py:91
  118.5 8.6 %while.66 = (s32[]{:T(128)}, f32[96,2,4,8]{3,0,2,1:T(8,128)S(1)}, f32[96,2,4,8]{3,0,2,1:T(8,128)S(1)}, f32[96,2,4,8,128]{4,3,2,0,1:T(8,128)}, s32[]{:T(128)}, /*...) while((s32[]{:T(128)}, f32[96,2,4,8]{3,0,2,1:T(8,128)S(1)}, ...), condition=%wide.region_8.8_spmd, body=%wide.region_5.7_spmd.sunk | while | flops 1086586880 | bytes 54109008 | solution.py:91
  133.0 8.6 %while.66 = (s32[]{:T(128)}, f32[96,2,4,8]{3,0,2,1:T(8,128)S(1)}, f32[96,2,4,8]{3,0,2,1:T(8,128)S(1)}, f32[96,2,4,8,128]{4,3,2,0,1:T(8,128)}, s32[]{:T(128)}, /*...) while((s32[]{:T(128)}, f32[96,2,4,8]{3,0,2,1:T(8,128)S(1)}, ...), condition=%wide.region_8.8_spmd, body=%wide.region_5.7_spmd.sunk | while | flops 1086586880 | bytes 54109008 | solution.py:91
  147.4 8.6 %while.66 = (s32[]{:T(128)}, f32[96,2,4,8]{3,0,2,1:T(8,128)S(1)}, f32[96,2,4,8]{3,0,2,1:T(8,128)S(1)}, f32[96,2,4,8,128]{4,3,2,0,1:T(8,128)}, s32[]{:T(128)}, /*...) while((s32[]{:T(128)}, f32[96,2,4,8]{3,0,2,1:T(8,128)S(1)}, ...), condition=%wide.region_8.8_spmd, body=%wide.region_5.7_spmd.sunk | while | flops 1086586880 | bytes 54109008 | solution.py:91
  161.9 8.6 %while.66 = (s32[]{:T(128)}, f32[96,2,4,8]{3,0,2,1:T(8,128)S(1)}, f32[96,2,4,8]{3,0,2,1:T(8,128)S(1)}, f32[96,2,4,8,128]{4,3,2,0,1:T(8,128)}, s32[]{:T(128)}, /*...) while((s32[]{:T(128)}, f32[96,2,4,8]{3,0,2,1:T(8,128)S(1)}, ...), condition=%wide.region_8.8_spmd, body=%wide.region_5.7_spmd.sunk | while | flops 1086586880 | bytes 54109008 | solution.py:91
  171.5 2.8 gather_fusion.3
  176.0 26.3 %pmax.7 = bf16[64,2,4,8]{3,2,1,0:T(4,128)(2,1)} all-reduce(bf16[64,2,4,8]{3,2,1,0:T(4,128)(2,1)} %select_convert_fusion), channel_id=1, replica_groups=mesh['seq'=8,'head'=4] {'seq'}, use_global_device_ids=true, to_apply=%region_10.12 | all-reduce | flops 4096 | bytes 16384 | tf_op jit(solution)/shard_map/pmax | solution.py:100
  205.9 2.5 gather_fusion.1
  211.7 4.7 %fusion.43 = (bf16[1,8,512,2,128]{4,3,2,1,0:T(2,128)(2,1)S(1)}, bf16[1,8,512,2,128]{4,3,2,1,0:T(2,128)(2,1)S(1)}) fusion(bf16[2,8,512,2,128]{4,3,2,1,0:T(2,128)(2,1)} %param.20), kind=kLoop, calls=%fused_computation.83 | loop fusion | bytes 8388608 | tf_op jit(solution)/shard_map/slice | solution.py:142
  218.7 30.3 %all-reduce.2 = bf16[64,2,4,8]{3,2,1,0:T(4,128)(2,1)} all-reduce(bf16[64,2,4,8]{3,2,1,0:T(4,128)(2,1)S(1)} %get-tuple-element.497), channel_id=4, replica_groups=mesh['seq'=8,'head'=4] {'seq'}, use_global_device_ids=true, to_apply=%region_14.16.clone | all-reduce | flops 4096 | bytes 16384
  252.1 30.3 %reduce-scatter.3.cloned.1.call-done = bf16[8,2,4,8,128]{4,3,2,1,0:T(8,128)(2,1)} async-done(((bf16[64,2,4,8,128]{4,3,2,1,0:T(8,128)(2,1)}), bf16[8,2,4,8,128]{4,3,2,1,0:T(8,128)(2,1)}) %reduce-scatter.3.cloned.1.call-update) | async-done | bytes 131088 | tf_op jit(solution)/shard_map/reduce_scatter | solution.py:106
  284.9 9.8 %gather_fusion.2 = bf16[256,1024]{1,0:T(8,128)(2,1)S(1)} fusion(bf16[16384,1024]{1,0:T(8,128)(2,1)} %param.24, s32[1024]{0:T(1024)S(1)} %pad_clamp_fusion), kind=kCustom, calls=%fused_computation.4 | custom fusion | bytes 1049600 | tf_op jit(solution)/shard_map/jit(_take)/gather | solution.py:161
  294.9 29.6 %all-gather.6.cloned.1.call-done = bf16[64,2,4,8,128]{4,3,2,1,0:T(8,128)(2,1)} async-done(((bf16[8,2,4,8,128]{4,3,2,1,0:T(8,128)(2,1)}), bf16[64,2,4,8,128]{4,3,2,1,0:T(8,128)(2,1)}) %all-gather.6.cloned.1.call-update) | async-done | bytes 1048592 | tf_op jit(solution)/shard_map/all_gather | solution.py:152
  324.5 5.2 %fusion.24 = bf16[64,4,1024]{2,0,1:T(8,128)(2,1)} fusion(bf16[2,8,128,1024,1]{3,2,1,0,4:T(8,128)(2,1)} %bitcast.124, bf16[64,2,4,8,128]{4,3,2,1,0:T(8,128)(2,1)} %all-gather.6.cloned.1.call-done, bf16[64,4,1024]{2,1,0:T(4,128)(2,1)S(1)} %reshape.143, pred[64,4]{0,1:T(4,128)(4,1)S(1)} %get-tuple-element.493, pred[64,4]{0,1:T(4,128)(4,1)S(1)} %get-tuple-element.511), kind=kOutput, calls=%fused_computation.37 | convolution fusion | flops 1075052544 | bytes 6291968 | tf_op jit(solution)/shard_map/rctgd,cgde->rte/dot_general | solution.py:156
  329.7 21.8 %reduce-scatter.5.cloned.1.call-done = bf16[16,4,1024]{2,0,1:T(8,128)(2,1)} async-done(((bf16[64,4,1024]{2,0,1:T(8,128)(2,1)}), bf16[16,4,1024]{2,0,1:T(8,128)(2,1)}) %reduce-scatter.5.cloned.1.call-update) | async-done | bytes 131088 | tf_op jit(solution)/shard_map/reduce_scatter | solution.py:164
  (206 shorter events, 124.2 us)
Async XLA Ops:
  6.5 43.3 %all-gather.4.cloned.1.call-start = ((), (), s32[]{:S(2)}) async-start(), calls=%async_computation.2 | async-start | bytes 1179648 | tf_op jit(solution)/shard_map/all_gather | solution.py:27
  7.3 275.1 %reduce-scatter.3.cloned.1.call-start = ((), (), s32[]{:S(2)}) async-start(), calls=%async_computation.3 | async-start | bytes 1179648 | tf_op jit(solution)/shard_map/reduce_scatter | solution.py:106
  54.8 119.5 %copy-start.10 = (pred[64]{0:T(512)(128)(4,1)S(1)}, pred[64]{0:T(512)(128)(4,1)}, u32[]{:S(2)}) copy-start(pred[64]{0:T(512)(128)(4,1)} %compare_and_fusion.3) | copy-start | bytes 196
  62.6 2.0 copy-start
  77.1 2.0 copy-start
  91.5 2.0 copy-start
  106.0 2.0 copy-start
  120.5 2.0 copy-start
  124.9 1.7 copy-start.1
  135.0 2.0 copy-start
  149.4 2.0 copy-start
  163.9 2.0 copy-start
  170.8 33.3 %copy-start.2 = (f32[96,2,4,8,128]{4,3,2,0,1:T(8,128)S(1)}, f32[96,2,4,8,128]{4,3,2,0,1:T(8,128)}, u32[]{:S(2)}) copy-start(f32[96,2,4,8,128]{4,3,2,0,1:T(8,128)} %get-tuple-element.407) | copy-start | bytes 9437188
  205.9 2.5 copy-start.3
  205.9 2.5 copy-start.4
  205.9 2.5 copy-start.5
  208.4 2.0 copy-start.12
  210.4 114.1 %all-gather.6.cloned.1.call-start = ((), (), s32[]{:S(2)}) async-start(), calls=%async_computation.4 | async-start | bytes 1179648 | tf_op jit(solution)/shard_map/all_gather | solution.py:152
  211.7 4.8 %copy-start.6 = (bf16[4,8,16,128]{3,2,1,0:T(8,128)(2,1)S(1)}, bf16[4,8,16,128]{3,2,1,0:T(8,128)(2,1)}, u32[]{:S(2)}) copy-start(bf16[4,8,16,128]{3,2,1,0:T(8,128)(2,1)} %param.16) | copy-start | bytes 393220
  211.7 4.8 %copy-start.9 = (pred[8,512]{1,0:T(8,128)(4,1)S(1)}, pred[8,512]{1,0:T(8,128)(4,1)}, u32[]{:S(2)}) copy-start(pred[8,512]{1,0:T(8,128)(4,1)} %iota_compare_fusion) | copy-start | bytes 12292
  216.5 33.4 %copy-start.7 = (f32[8,2,4,8,4]{3,4,2,1,0:T(4,128)S(1)}, f32[8,2,4,8,4]{3,4,2,1,0:T(4,128)}, u32[]{:S(2)}) copy-start(f32[8,2,4,8,4]{3,4,2,1,0:T(4,128)} %get-tuple-element.517) | copy-start | bytes 24580
  216.5 34.7 %copy-start.8 = (bf16[1,4,8,2,128]{4,3,2,1,0:T(2,128)(2,1)S(1)}, bf16[1,4,8,2,128]{4,3,2,1,0:T(2,128)(2,1)}, u32[]{:S(2)}) copy-start(bf16[1,4,8,2,128]{4,3,2,1,0:T(2,128)(2,1)} %get-tuple-element.509) | copy-start | bytes 49156
  250.0 34.7 %copy-start.11 = (s32[64,4]{0,1:T(4,128)S(1)}, s32[64,4]{0,1:T(4,128)}, u32[]{:S(2)}) copy-start(s32[64,4]{0,1:T(4,128)} %param.23) | copy-start | bytes 3076
  284.6 67.0 %reduce-scatter.5.cloned.1.call-start = ((), (), s32[]{:S(2)}) async-start(), calls=%async_computation.5 | async-start | bytes 655360 | tf_op jit(solution)/shard_map/reduce_scatter | solution.py:164
  (7 other events, 11.7 us)
Sparse Core Ops, SparseCore 0:
  9.5 40.2 all-gather.3
  210.5 71.8 reduce-scatter.2
  284.8 39.6 all-gather.5
  329.9 21.6 reduce-scatter.4
where the time goes:
time: 364 us; the launch traced here: 360 us
  waiting for transfers between devices  106 us (29%)
  local copies, waits for them, and re-layouts  84 us (23%)
  blocking collectives  63 us (17%)
  matrix products  42.3 us (12%)
  other arithmetic  29.5 us (8%)
  loops' own time  20.1 us (6%)
  between operations  14.7 us (4%)
    unnamed x1, blocking collectives  30.3 us
    reduce_scatter x1, waiting for transfers between devices, shards(): lax.psum_scatter((blended * factor[..., None]).astype(jnp.bfloat16), 'seq...  30.3 us
    all_gather x1, waiting for transfers between devices, shards(): attention_all = lax.all_gather(attention, 'seq', axis=0, tiled=True)  29.6 us
    pmax x1, blocking collectives, shards(): lax.pmax(highest.astype(jnp.bfloat16), 'seq').astype(highest.dtype)  26.3 us
    all_gather x1, waiting for transfers between devices, shards(): lax.all_gather(queries, 'seq', axis=1, tiled=True)  23.5 us
    dynamic_slice x16, local copies, waits for them, and re-layouts, per_prompt(): lax.dynamic_index_in_dim(prompt_values, prompt_index, 0, keepdims=False)  22.3 us
    reduce_scatter x1, waiting for transfers between devices, shards(): lax.psum_scatter((projected + jnp.where(inside[..., None], embedded, 0.0)...  21.8 us
    dot_general x8, matrix products, per_tile(): jnp.einsum('rctgk,kcd->rctgd', weights.astype(jnp.bfloat16), value_rows,...  18.9 us
  transfers between devices with their start and end apart: 4, of which 4 were waited for; matrix products, arithmetic and copies ran while one was open for 9% of the time, Pallas kernels for 0%

commit v1 on v0

v1 whole, which is shorter than its diff:
```python
import functools
import math

import jax
import jax.numpy as jnp
from jax import lax
from jax.experimental import pallas as pl
from jax.experimental.pallas import tpu as pltpu
from jax.sharding import PartitionSpec as P

MESH = pl.DeviceIdType.MESH
F32 = jnp.float32
BF16 = jnp.bfloat16
NT = (((1,), (1,)), ((), ()))
VMEM_BYTES = 58 * 2**20


def split_axis(n):
    inner = 2 if n <= 8 else 8
    return n // inner, inner


def greet(peers):
    barrier = pltpu.get_barrier_semaphore()
    for peer in peers:
        pl.semaphore_signal(barrier, inc=1, device_id=peer, device_id_type=MESH)
    pl.semaphore_wait(barrier, len(peers))


def seq_peers(n, me):
    outer, inner = split_axis(n)
    a, b = me // inner, lax.rem(me, inner)
    line = [lax.rem(a + k, outer) * inner + b for k in range(outer)]
    side = [a * inner + lax.rem(b + j, inner) for j in range(inner)]
    return line, side


class Gather:
    def __init__(self, n, me, bufs, send1, recv1, send2, recv2):
        self.n, self.me, self.bufs = n, me, bufs
        self.outer, self.inner = split_axis(n)
        self.sems = (send1, recv1, send2, recv2)
        self.a, self.b = me // self.inner, lax.rem(me, self.inner)
        self.sent = []

    def shard(self, k, j):
        a = lax.rem(self.a - k + self.outer, self.outer)
        b = lax.rem(self.b - j + self.inner, self.inner)
        return a * self.inner + b

    def copy1(self, i, k, shard):
        send1, recv1, _, _ = self.sems
        peer = lax.rem(self.a + k, self.outer) * self.inner + self.b
        buf = self.bufs[i]
        return pltpu.make_async_remote_copy(
            src_ref=buf.at[shard], dst_ref=buf.at[shard], send_sem=send1.at[i, k], recv_sem=recv1.at[i, k],
            device_id={"seq": peer}, device_id_type=MESH)

    def copy2(self, i, k, j, shard):
        _, _, send2, recv2 = self.sems
        peer = self.a * self.inner + lax.rem(self.b + j, self.inner)
        buf = self.bufs[i]
        return pltpu.make_async_remote_copy(
            src_ref=buf.at[shard], dst_ref=buf.at[shard], send_sem=send2.at[i, k, j], recv_sem=recv2.at[i, k, j],
            device_id={"seq": peer}, device_id_type=MESH)

    def begin(self, copy):
        copy.start()
        self.sent.append(copy)

    def start(self):
        for k in range(1, self.outer):
            for i in range(len(self.bufs)):
                self.begin(self.copy1(i, k, self.me))
        self.forward(0)

    def forward(self, k):
        shard = self.shard(k, 0)
        for i in range(len(self.bufs)):
            if k:
                self.copy1(i, k, shard).wait_recv()
            for j in range(1, self.inner):
                self.begin(self.copy2(i, k, j, shard))

    def finish(self):
        for k in range(self.outer):
            for j in range(1, self.inner):
                for i in range(len(self.bufs)):
                    self.copy2(i, k, j, self.shard(k, j)).wait_recv()
        for copy in self.sent:
            copy.wait_send()


def gather_sems(n, count):
    outer, inner = split_axis(n)
    line = pltpu.SemaphoreType.DMA((count, outer))
    side = pltpu.SemaphoreType.DMA((count, outer, inner))
    return [line, line, side, side]


def eye(rows, lanes=128):
    return lax.broadcasted_iota(jnp.int32, (rows, lanes), 0) == lax.broadcasted_iota(jnp.int32, (rows, lanes), 1)


def to_row(column):
    return jnp.sum(jnp.where(eye(column.shape[0]), column, 0.0), axis=0, keepdims=True)


def to_column(row, rows):
    return jnp.sum(jnp.where(eye(rows), row, 0.0), axis=1, keepdims=True)


def softmax_mix(scores, values, scale2):
    peak = jnp.max(scores, axis=-1, keepdims=True)
    weights = jnp.exp2((scores - peak) * scale2)
    total = jnp.sum(weights, axis=-1, keepdims=True)
    mixed = jnp.dot(weights.astype(BF16), values, preferred_element_type=F32)
    return mixed / total, peak * scale2 + jnp.log2(total)


def share_kernel(n, scale2, steps, lengths, q_own, ids_own, fresh, suffix, q_all, ids_all, mixed_ref, lse_ref,
                 raw, wide, keys, values, local_sem, send1, recv1, send2, recv2):
    rows, kv, queries, width = q_own.shape
    suf = suffix.shape[2] // kv
    live = keys.shape[1]
    me = lax.axis_index("seq")
    line, side = seq_peers(n, me)
    greet([{"seq": d} for d in line[1:] + side[1:]])
    q_all[me] = q_own[...]
    ids_all[me] = ids_own[...]
    gather = Gather(n, me, [q_all, ids_all], send1, recv1, send2, recv2)
    gather.start()
    load = pltpu.make_async_copy(suffix, raw, local_sem.at[0])
    load.start()
    keys[...] = jnp.zeros_like(keys)
    values[...] = jnp.zeros_like(values)
    column = lax.broadcasted_iota(jnp.int32, (queries, live), 1)
    step = lax.broadcasted_iota(jnp.int32, (queries, live), 0) // (queries // steps)
    new = jnp.logical_and(column >= suf, column - suf <= step)
    load.wait()

    def one_row(r, carry):
        old = column < lengths[r]
        stats = []
        for part, store in ((0, keys), (1, values)):
            wide[part] = raw[part, r].astype(F32)
            for c in range(kv):
                store[c, 0:suf] = wide[part, pl.ds(c, suf, stride=kv), :].astype(BF16)
                store[c, suf:suf + fresh.shape[3]] = fresh[part, r, c]
        for c in range(kv):
            scores = lax.dot_general(q_own[r, c], keys[c], NT, preferred_element_type=F32)
            scores = jnp.where(jnp.logical_or(old, new), scores, -jnp.inf)
            mixed, lse = softmax_mix(scores, values[c], scale2)
            mixed_ref[r, c * queries:(c + 1) * queries] = mixed
            stats.append(lse)
        lse_ref[pl.ds(r, 1), :] = to_row(jnp.concatenate(stats, axis=0))
        return carry

    outer = gather.outer
    for k in range(outer):
        lax.fori_loop(rows * k // outer, rows * (k + 1) // outer, one_row, 0)
        if k + 1 < outer:
            gather.forward(k + 1)
    gather.finish()


def prompt_kernel(scale2, tile, ids, local_ids, q_ref, k_ref, v_ref, rem_ref, embedding, o_ref, lse_ref, e_ref,
                  order, wide, keys, values, blocks, sem):
    p = pl.program_id(0)
    rows, kv, queries, width = q_ref.shape
    positions = k_ref.shape[1] // kv
    vocab = embedding.shape[0]
    tokens = rem_ref.shape[0]

    @pl.when(p == 0)
    def _():
        def fetch(i, carry):
            first = pl.multiple_of(jnp.clip(local_ids[i], 0, vocab - 1) // 16 * 16, 16)
            pltpu.make_async_copy(embedding.at[pl.ds(first, 16)], blocks.at[pl.ds(pl.multiple_of(i * 16, 16), 16)], sem.at[0]).start()
            return carry
        lax.fori_loop(0, tokens, fetch, 0)

    def scan(r, count):
        order[count] = r
        return count + (ids[r] == p).astype(jnp.int32)

    count = lax.fori_loop(0, rows, scan, 0)
    last = order[jnp.maximum(count - 1, 0)]
    for j in range(tile):
        order[count + j] = last
    for source, store, part in ((k_ref, keys, 0), (v_ref, values, 1)):
        wide[part] = source[0].astype(F32)
        for c in range(kv):
            store[c] = wide[part, pl.ds(c, positions, stride=kv), :].astype(BF16)

    def one_tile(i, carry):
        picked = [order[i * tile + j] for j in range(tile)]
        results = []
        for c in range(kv):
            query = jnp.concatenate([q_ref[r, c] for r in picked], axis=0)
            scores = lax.dot_general(query, keys[c], NT, preferred_element_type=F32)
            results.append(softmax_mix(scores, values[c], scale2))
        for j, r in enumerate(picked):
            span = slice(j * queries, (j + 1) * queries)
            for c in range(kv):
                o_ref[r, c * queries:(c + 1) * queries] = results[c][0][span].astype(BF16)
            lse_ref[pl.ds(r, 1), :] = to_row(jnp.concatenate([results[c][1][span] for c in range(kv)], axis=0))
        return carry

    lax.fori_loop(0, (count + tile - 1) // tile, one_tile, 0)

    @pl.when(p == pl.num_programs(0) - 1)
    def _():
        span = min(vocab, tokens * 16)
        for i in range(tokens * 16 // span):
            pltpu.make_async_copy(embedding.at[pl.ds(0, span)], blocks.at[pl.ds(i * span, span)], sem.at[0]).wait()
        lane = lax.broadcasted_iota(jnp.int32, (16, 256), 1)
        owner = lane // 16 == lax.broadcasted_iota(jnp.int32, (16, 256), 0)

        def pick(i, carry):
            rem = rem_ref[pl.ds(pl.multiple_of(i * 16, 16), 16), 0:1]
            chosen = jnp.logical_and(owner, lax.rem(lane, 16) == rem).astype(F32).astype(BF16)
            block = blocks[pl.ds(pl.multiple_of(i * 256, 256), 256), :]
            e_ref[pl.ds(pl.multiple_of(i * 16, 16), 16), :] = jnp.dot(chosen, block, preferred_element_type=F32).astype(BF16)
            return carry
        lax.fori_loop(0, tokens // 16, pick, 0)


def finish_kernel(n, heads_n, steps, kv, o_ref, lse_ref, s_ref, s_lse, e_ref, weight, out_ref,
                  side_o, side_l, line_o, line_l, pass_o, pass_l, share, flat, att_all, w_buf, part, landed,
                  local_sem, so1, ro1, sl1, rl1, so2, ro2, sl2, rl2, gs1, gr1, gs2, gr2, hs, hr):
    rows, queries, width = s_ref.shape
    outer, inner = split_axis(n)
    me = lax.axis_index("seq")
    head = lax.axis_index("head")
    line, side = seq_peers(n, me)
    a, b = me // inner, lax.rem(me, inner)
    load = pltpu.make_async_copy(weight, w_buf, local_sem.at[0])
    load.start()
    greet([{"seq": d} for d in line[1:] + side[1:]] + [{"head": lax.rem(head + i, heads_n)} for i in range(1, heads_n)])
    order = list(range(1, outer)) + [0]

    def remote(src, dst, send, recv, **to):
        return pltpu.make_async_remote_copy(src_ref=src, dst_ref=dst, send_sem=send, recv_sem=recv, device_id=to, device_id_type=MESH)

    def side_copies(k, j):
        shard = lax.rem(a + k, outer) * inner + lax.rem(b + j, inner)
        return [remote(o_ref.at[shard], side_o.at[k, j], so1.at[k, j], ro1.at[k, j], seq=side[j]),
                remote(lse_ref.at[shard], side_l.at[k, j], sl1.at[k, j], rl1.at[k, j], seq=side[j])]

    def line_copies(k):
        return [remote(pass_o.at[k], line_o.at[k], so2.at[k], ro2.at[k], seq=line[k]),
                remote(pass_l.at[k], line_l.at[k], sl2.at[k], rl2.at[k], seq=line[k])]

    sent = []
    for k in order:
        for j in range(1, inner):
            for copy in side_copies(k, j):
                copy.start()
                sent.append(copy)

    def blend(lses, read, write):
        peak = functools.reduce(jnp.maximum, lses)
        raw = [jnp.exp2(l - peak) for l in lses]
        total = functools.reduce(jnp.add, raw)
        for i, w in enumerate(raw):
            share[i] = w / total

        def one_row(r, carry):
            mixed = None
            for i in range(len(lses)):
                term = to_column(share[i, pl.ds(r, 1), :], queries) * read(i, r).astype(F32)
                mixed = term if mixed is None else mixed + term
            write(r, mixed)
            return carry

        lax.fori_loop(0, rows, one_row, 0)
        return peak + jnp.log2(total)

    for k in order:
        own = lax.rem(a + k, outer) * inner + b
        for j in range(1, inner):
            for copy in side_copies(k, j):
                copy.wait_recv()

        def read(i, r, k=k, own=own):
            return o_ref[own, r] if i == 0 else side_o[k, i, r]

        def write(r, mixed, k=k):
            pass_o[k, r] = mixed.astype(BF16)

        lses = [lse_ref[own]] + [side_l[k, j] for j in range(1, inner)]
        pass_l[k] = blend(lses, read, write)
        if k:
            for copy in line_copies(k):
                copy.start()
                sent.append(copy)
    for k in range(1, outer):
        for copy in line_copies(k):
            copy.wait_recv()

    def read(i, r):
        if i == outer:
            return s_ref[r]
        return pass_o[0, r] if i == 0 else line_o[i, r]

    group = queries // (kv * steps)

    def write(r, mixed):
        for c in range(kv):
            for t in range(steps):
                first = pl.multiple_of((r * steps + t) * (kv * group) + c * group, group)
                at = (c * steps + t) * group
                flat[pl.ds(first, group), :] = mixed[at:at + group]

    blend([pass_l[0]] + [line_l[k] for k in range(1, outer)] + [s_lse[...]], read, write)
    heads = kv * group
    for h in range(heads):
        att_all[me, :, h * width:(h + 1) * width] = flat[pl.ds(h, rows * steps, stride=heads), :].astype(BF16)
    gather = Gather(n, me, [att_all], gs1, gr1, gs2, gr2)
    gather.start()
    for k in range(1, outer):
        gather.forward(k)
    load.wait()
    gather.finish()

    columns = part.shape[2]
    tile = 256
    total_rows = n * rows * steps

    def project(i, carry):
        cols = pl.ds(pl.multiple_of(i * tile, tile), tile)
        lhs = att_all[...].reshape(total_rows, att_all.shape[2])
        done = jnp.dot(lhs, w_buf[:, cols], preferred_element_type=F32) + e_ref[:, cols].astype(F32)
        part[:, :, cols] = done.astype(BF16).reshape(heads_n, total_rows // heads_n, tile)
        return carry

    lax.fori_loop(0, columns // tile, project, 0)

    def head_copy(i):
        peer = lax.rem(head + i, heads_n)
        return remote(part.at[peer], landed.at[i], hs.at[i], hr.at[i], head=peer)

    for i in range(1, heads_n):
        copy = head_copy(i)
        copy.start()
        sent.append(copy)
    for i in range(1, heads_n):
        head_copy(i).wait_recv()
    total = part[head].astype(F32)
    for i in range(1, heads_n):
        total = total + landed[i].astype(F32)
    out_ref[...] = total.astype(BF16)
    for copy in sent:
        copy.wait_send()


def vmem():
    return pl.BlockSpec(memory_space=pltpu.VMEM)


def shards(n, heads_n, queries, new_kv, prompt_keys, prompt_values, suffix_kv, prompt_ids, suffix_lengths,
           token_ids, embedding, out_weight):
    steps, rows, heads, width = queries.shape
    prompts, positions, kv, _ = prompt_keys.shape
    group = heads // kv
    per = steps * group
    suf = suffix_kv.shape[2]
    all_rows = n * rows
    outer, inner = split_axis(n)
    scale2 = width ** -0.5 * math.log2(math.e)
    sds = jax.ShapeDtypeStruct
    dma = pltpu.SemaphoreType.DMA

    q_own = queries.reshape(steps, rows, kv, group, width).transpose(1, 2, 0, 3, 4).reshape(rows, kv, per, width)
    ids_own = jnp.broadcast_to(prompt_ids, (rows, 128))
    fresh = jnp.pad(new_kv.transpose(0, 2, 3, 1, 4), ((0, 0), (0, 0), (0, 0), (0, 16 - steps), (0, 0)))
    live = suf + 128
    q_all, ids_all, s_mixed, s_lse = pl.pallas_call(
        functools.partial(share_kernel, n, scale2, steps),
        out_shape=(sds((n, rows, kv, per, width), BF16), sds((n, rows, 128), jnp.int32),
                   sds((rows, kv * per, width), F32), sds((rows, 128), F32)),
        in_specs=[pl.BlockSpec(memory_space=pltpu.SMEM), vmem(), vmem(), vmem(), pl.BlockSpec(memory_space=pl.ANY)],
        out_specs=(vmem(),) * 4,
        scratch_shapes=[
            pltpu.VMEM((2, rows, suf * kv, width), BF16), pltpu.VMEM((2, suf * kv, width), F32),
            pltpu.VMEM((kv, live, width), BF16), pltpu.VMEM((kv, live, width), BF16), dma((1,)),
            *gather_sems(n, 2)],
        compiler_params=pltpu.CompilerParams(collective_id=0, has_side_effects=True, vmem_limit_bytes=VMEM_BYTES),
        name="share_queries",
    )(suffix_lengths.astype(jnp.int32), q_own, ids_own, fresh, suffix_kv.reshape(2, rows, suf * kv, width))

    tokens = all_rows * steps
    vocab = embedding.shape[0]
    local_ids = token_ids.reshape(tokens) - lax.axis_index("head") * vocab
    inside = (local_ids >= 0) & (local_ids < vocab)
    rem = jnp.broadcast_to(jnp.where(inside, local_ids % 16, -1)[:, None], (tokens, 128))
    tile = 4
    fixed = lambda *shape: pl.BlockSpec(shape, lambda p, *_: (0,) * len(shape))
    cut = pl.BlockSpec((1, positions * kv, width), lambda p, *_: (p, 0, 0))
    o_all, lse_all, embedded = pl.pallas_call(
        functools.partial(prompt_kernel, scale2, tile),
        out_shape=(sds((all_rows, kv * per, width), BF16), sds((all_rows, 128), F32), sds((tokens, embedding.shape[1]), BF16)),
        grid_spec=pltpu.PrefetchScalarGridSpec(
            num_scalar_prefetch=2, grid=(prompts,),
            in_specs=[fixed(all_rows, kv, per, width), cut, cut, fixed(tokens, 128), pl.BlockSpec(memory_space=pl.ANY)],
            out_specs=(fixed(all_rows, kv * per, width), fixed(all_rows, 128), fixed(tokens, embedding.shape[1])),
            scratch_shapes=[
                pltpu.SMEM((all_rows + tile,), jnp.int32), pltpu.VMEM((2, positions * kv, width), F32),
                pltpu.VMEM((kv, positions, width), BF16), pltpu.VMEM((kv, positions, width), BF16),
                pltpu.VMEM((tokens * 16, embedding.shape[1]), BF16), dma((1,))]),
        compiler_params=pltpu.CompilerParams(vmem_limit_bytes=VMEM_BYTES),
        name="prompt_attention",
    )(ids_all[:, :, 0].reshape(all_rows), local_ids, q_all.reshape(all_rows, kv, per, width),
      prompt_keys.reshape(prompts, positions * kv, width), prompt_values.reshape(prompts, positions * kv, width), rem, embedding)

    columns = out_weight.shape[1]
    out_rows = tokens // heads_n
    pair = dma((outer, inner))
    out = pl.pallas_call(
        functools.partial(finish_kernel, n, heads_n, steps, kv),
        out_shape=sds((out_rows, columns), BF16),
        in_specs=[vmem()] * 5 + [pl.BlockSpec(memory_space=pl.ANY)],
        out_specs=vmem(),
        scratch_shapes=[
            pltpu.VMEM((outer, inner, rows, kv * per, width), BF16), pltpu.VMEM((outer, inner, rows, 128), F32),
            pltpu.VMEM((outer, rows, kv * per, width), BF16), pltpu.VMEM((outer, rows, 128), F32),
            pltpu.VMEM((outer, rows, kv * per, width), BF16), pltpu.VMEM((outer, rows, 128), F32),
            pltpu.VMEM((max(inner, outer + 1), rows, 128), F32), pltpu.VMEM((rows * kv * per, width), F32),
            pltpu.VMEM((n, rows * steps, heads * width), BF16), pltpu.VMEM(out_weight.shape, BF16),
            pltpu.VMEM((heads_n, out_rows, columns), BF16), pltpu.VMEM((heads_n, out_rows, columns), BF16),
            dma((1,)), pair, pair, pair, pair, dma((outer,)), dma((outer,)), dma((outer,)), dma((outer,)),
            *gather_sems(n, 1), dma((heads_n,)), dma((heads_n,))],
        compiler_params=pltpu.CompilerParams(collective_id=1, has_side_effects=True, vmem_limit_bytes=VMEM_BYTES),
        name="finish",
    )(o_all.reshape(n, rows, kv * per, width), lse_all.reshape(n, rows, 128), s_mixed, s_lse, embedded, out_weight)
    return out.reshape(all_rows // heads_n, steps, columns)


def solution(mesh):
    return jax.shard_map(
        functools.partial(shards, mesh.shape["seq"], mesh.shape["head"]),
        mesh=mesh,
        in_specs=(
            P(None, "seq", "head", None),
            P(None, None, "seq", "head", None),
            P(None, "seq", "head", None),
            P(None, "seq", "head", None),
            P(None, "seq", None, "head", None),
            P("seq", None),
            P("seq"),
            P(),
            P("head", "seq"),
            P("head", "seq"),
        ),
        out_specs=P("head", None, "seq"),
        check_vma=False,
    )
```

time: 364 us -> 128 us (0.35)
  the two profiles are of different devices: /device:TPU:21 before, /device:TPU:17 now
where the time goes in v1:
time: 128 us; the launch traced here: 127 us
  Pallas kernels  118 us (92%)
  local copies, waits for them, and re-layouts  7.58 us (6%)
    pallas_call x1, Pallas kernels, shards(): pl.pallas_call(functools.partial(finish_kernel, n, heads_n, steps, kv), o...  66.8 us
    pallas_call x1, Pallas kernels, shards(): pl.pallas_call(functools.partial(prompt_kernel, scale2, tile), out_shape=...  34.5 us
    pallas_call x1, Pallas kernels, shards(): pl.pallas_call(functools.partial(share_kernel, n, scale2, steps), out_sha...  17.1 us

profile of v1, /device:TPU:17, one launch (start us, length us, event | category | flops | bytes accessed | tf_op | source)
XLA Modules:
  0.0 126.7 jit_solution(5460769274542416375)
XLA Ops:
  0.0 0.0 copy-start
  0.0 0.7 broadcast_subtract_fusion
  0.7 1.3 %broadcast_in_dim.18.ids_own = s32[8,128]{1,0:T(8,128)} broadcast(s32[8]{0:T(128)} %bitcast.24), dimensions={0} | broadcast | bytes 4128 | tf_op jit(solution)/shard_map/broadcast_in_dim | solution.py:376
  2.0 0.1 copy.15
  2.1 0.1 sub.10.local_ids
  2.2 0.0 copy-start.1
  2.3 0.8 copy.18
  3.0 0.7 pad.4.fresh
  3.7 0.8 broadcast_in_dim.20.rem_ref
  4.5 0.0 copy-done
  4.5 0.7 copy_bitcast_fusion.q_own
  5.1 17.1 %share_queries.1 = (bf16[8,8,2,32,128]{4,3,2,1,0:T(8,128)(2,1)}, s32[8,8,128]{2,1,0:T(8,128)}, f32[8,64,128]{2,1,0:T(8,128)}, f32[8,128]{1,0:T(8,128)}) custom-call(s32[8]{0:T(128)} %lengths.1, bf16[8,2,32,128]{3,2,1,0:T(8,128)(2,1)} %copy_bitcast_fusion.q_own, s32[8,128]{1,0:T(8,128)} %broadcast_in_dim.18.ids_own, bf16[2,8,2,16,128]{4,3,2,1,0:T(8,128)(2,1)} %pad.4.fresh, ...), custom_call_target="tpu_custom_call" | custom-call | tf_op jit(solution)/shard_map/share_queries/pallas_call | solution.py:379
  22.2 1.0 slice_reduce_fusion
  23.2 0.6 reshape_squeeze.3.ids
  23.8 0.0 copy-done.1
  23.8 34.5 %prompt_attention.1 = (bf16[64,64,128]{2,1,0:T(8,128)(2,1)}, f32[64,128]{1,0:T(8,128)}, bf16[256,1024]{1,0:T(8,128)(2,1)}) custom-call(s32[64]{0:T(128)} %reshape_squeeze.3.ids, s32[256]{0:T(256)} %copy-done.1, bf16[64,2,32,128]{3,2,1,0:T(8,128)(2,1)} %bitcast.20, bf16[8,2048,128]{2,1,0:T(8,128)(2,1)} %bitcast.17, bf16[8,2048,128]{2,1,0:T(8,128)(2,1)} %bitcast.18, ...), custom_call_target="tpu_custom_call" | custom-call | tf_op jit(solution)/shard_map/prompt_attention/pallas_call | solution.py:401
  58.3 66.8 %finish.1 = bf16[64,1024]{1,0:T(8,128)(2,1)} custom-call(bf16[8,8,64,128]{3,2,1,0:T(8,128)(2,1)} %bitcast.21, f32[8,8,128]{2,1,0:T(8,128)} %bitcast.23, f32[8,64,128]{2,1,0:T(8,128)} %get-tuple-element.16.s_ref, f32[8,128]{1,0:T(8,128)} %get-tuple-element.17.s_lse, bf16[256,1024]{1,0:T(8,128)(2,1)} %get-tuple-element.18.e_ref, bf16[2048,1024]{1,0:T(8,128)(2,1)} %weight.1), custom_call_target="tpu_custom_call" | custom-call | tf_op jit(solution)/shard_map/finish/pallas_call | solution.py:420
  125.1 1.6 %reshape.58 = bf16[16,4,1024]{2,1,0:T(4,128)(2,1)} reshape(bf16[64,1024]{1,0:T(8,128)(2,1)} %finish.1) | data formatting | bytes 262144 | tf_op jit(solution)/shard_map/reshape | solution.py:437
  (1 shorter events, 0.0 us)
Async XLA Ops:
  0.0 4.5 %copy-start = (bf16[4,8,16,128]{3,2,1,0:T(8,128)(2,1)S(1)}, bf16[4,8,16,128]{3,2,1,0:T(8,128)(2,1)}, u32[]{:S(2)}) copy-start(bf16[4,8,16,128]{3,2,1,0:T(8,128)(2,1)} %param.10) | copy-start | bytes 393220
  2.2 21.5 %copy-start.1 = (s32[256]{0:T(256)}, s32[256]{0:T(256)S(1)}, u32[]{:S(2)}) copy-start(s32[256]{0:T(256)S(1)} %sub.10.local_ids) | copy-start | bytes 3076

commit v2 on v1

--- a/solution.py
+++ b/solution.py
@@ -110,15 +110,14 @@
     return jnp.sum(jnp.where(eye(rows), row, 0.0), axis=1, keepdims=True)
 
 
-def softmax_mix(scores, values, scale2):
+def weigh(scores, scale2):
     peak = jnp.max(scores, axis=-1, keepdims=True)
     weights = jnp.exp2((scores - peak) * scale2)
     total = jnp.sum(weights, axis=-1, keepdims=True)
-    mixed = jnp.dot(weights.astype(BF16), values, preferred_element_type=F32)
-    return mixed / total, peak * scale2 + jnp.log2(total)
-
-
-def share_kernel(n, scale2, steps, lengths, q_own, ids_own, fresh, suffix, q_all, ids_all, mixed_ref, lse_ref,
+    return weights.astype(BF16), 1.0 / total, peak * scale2 + jnp.log2(total)
+
+
+def share_kernel(n, scale2, steps, lengths, prompt_ids, q_own, fresh, suffix, q_all, ids_all, mixed_ref, lse_ref,
                  raw, wide, keys, values, local_sem, send1, recv1, send2, recv2):
     rows, kv, queries, width = q_own.shape
     suf = suffix.shape[2] // kv
@@ -127,7 +126,11 @@
     line, side = seq_peers(n, me)
     greet([{"seq": d} for d in line[1:] + side[1:]])
     q_all[me] = q_own[...]
-    ids_all[me] = ids_own[...]
+    sublane = lax.broadcasted_iota(jnp.int32, (rows, 128), 0)
+    ids_own = jnp.zeros((rows, 128), jnp.int32)
+    for r in range(rows):
+        ids_own = jnp.where(sublane == r, prompt_ids[r, 0], ids_own)
+    ids_all[me] = ids_own
     gather = Gather(n, me, [q_all, ids_all], send1, recv1, send2, recv2)
     gather.start()
     load = pltpu.make_async_copy(suffix, raw, local_sem.at[0])
@@ -147,11 +150,12 @@
             for c in range(kv):
                 store[c, 0:suf] = wide[part, pl.ds(c, suf, stride=kv), :].astype(BF16)
                 store[c, suf:suf + fresh.shape[3]] = fresh[part, r, c]
-        for c in range(kv):
-            scores = lax.dot_general(q_own[r, c], keys[c], NT, preferred_element_type=F32)
-            scores = jnp.where(jnp.logical_or(old, new), scores, -jnp.inf)
-            mixed, lse = softmax_mix(scores, values[c], scale2)
-            mixed_ref[r, c * queries:(c + 1) * queries] = mixed
+        seen = jnp.logical_or(old, new)
+        scores = [lax.dot_general(q_own[r, c], keys[c], NT, preferred_element_type=F32) for c in range(kv)]
+        weighed = [weigh(jnp.where(seen, x, -jnp.inf), scale2) for x in scores]
+        for c, (weights, inverse, lse) in enumerate(weighed):
+            mixed = jnp.dot(weights, values[c], preferred_element_type=F32)
+            mixed_ref[r, c * queries:(c + 1) * queries] = mixed * inverse
             stats.append(lse)
         lse_ref[pl.ds(r, 1), :] = to_row(jnp.concatenate(stats, axis=0))
         return carry
@@ -164,47 +168,66 @@
     gather.finish()
 
 
-def prompt_kernel(scale2, tile, ids, local_ids, q_ref, k_ref, v_ref, rem_ref, embedding, o_ref, lse_ref, e_ref,
-                  order, wide, keys, values, blocks, sem):
+def prompt_kernel(scale2, tile, tokens_ref, ids, q_ref, k_ref, v_ref, embedding, o_ref, lse_ref, blocks,
+                  order, counts, wide, keys, values, sem):
     p = pl.program_id(0)
+    prompts = counts.shape[0]
     rows, kv, queries, width = q_ref.shape
     positions = k_ref.shape[1] // kv
     vocab = embedding.shape[0]
-    tokens = rem_ref.shape[0]
+    token_rows, steps = tokens_ref.shape
+    tokens = token_rows * steps
+    room = rows + tile
 
     @pl.when(p == 0)
     def _():
-        def fetch(i, carry):
-            first = pl.multiple_of(jnp.clip(local_ids[i], 0, vocab - 1) // 16 * 16, 16)
-            pltpu.make_async_copy(embedding.at[pl.ds(first, 16)], blocks.at[pl.ds(pl.multiple_of(i * 16, 16), 16)], sem.at[0]).start()
+        first_id = lax.axis_index("head") * vocab
+
+        def fetch(r, carry):
+            for t in range(steps):
+                local = jnp.clip(tokens_ref[r, t] - first_id, 0, vocab - 1)
+                first = pl.multiple_of(local // 16 * 16, 16)
+                to = pl.multiple_of((r * steps + t) * 16, 16)
+                pltpu.make_async_copy(embedding.at[pl.ds(first, 16)], blocks.at[pl.ds(to, 16)], sem.at[0]).start()
             return carry
-        lax.fori_loop(0, tokens, fetch, 0)
-
-    def scan(r, count):
-        order[count] = r
-        return count + (ids[r] == p).astype(jnp.int32)
-
-    count = lax.fori_loop(0, rows, scan, 0)
-    last = order[jnp.maximum(count - 1, 0)]
+
+        for i in range(prompts):
+            counts[i] = 0
+
+        def place(r, carry):
+            mine = ids[r, 0]
+            count = counts[mine]
+            order[mine * room + count] = r
+            counts[mine] = count + 1
+            return carry
+
+        lax.fori_loop(0, token_rows, fetch, 0)
+        lax.fori_loop(0, rows, place, 0)
+
+    count = counts[p]
+    base = p * room
+    last = order[base + jnp.maximum(count - 1, 0)]
     for j in range(tile):
-        order[count + j] = last
+        order[base + count + j] = last
     for source, store, part in ((k_ref, keys, 0), (v_ref, values, 1)):
         wide[part] = source[0].astype(F32)
         for c in range(kv):
             store[c] = wide[part, pl.ds(c, positions, stride=kv), :].astype(BF16)
 
     def one_tile(i, carry):
-        picked = [order[i * tile + j] for j in range(tile)]
-        results = []
+        picked = [order[base + i * tile + j] for j in range(tile)]
+        scores = []
         for c in range(kv):
             query = jnp.concatenate([q_ref[r, c] for r in picked], axis=0)
-            scores = lax.dot_general(query, keys[c], NT, preferred_element_type=F32)
-            results.append(softmax_mix(scores, values[c], scale2))
+            scores.append(lax.dot_general(query, keys[c], NT, preferred_element_type=F32))
+        weighed = [weigh(x, scale2) for x in scores]
+        for c, (weights, inverse, _) in enumerate(weighed):
+            mixed = (jnp.dot(weights, values[c], preferred_element_type=F32) * inverse).astype(BF16)
+            for j, r in enumerate(picked):
+                o_ref[r, c * queries:(c + 1) * queries] = mixed[j * queries:(j + 1) * queries]
         for j, r in enumerate(picked):
             span = slice(j * queries, (j + 1) * queries)
-            for c in range(kv):
-                o_ref[r, c * queries:(c + 1) * queries] = results[c][0][span].astype(BF16)
-            lse_ref[pl.ds(r, 1), :] = to_row(jnp.concatenate([results[c][1][span] for c in range(kv)], axis=0))
+            lse_ref[pl.ds(r, 1), :] = to_row(jnp.concatenate([w[2][span] for w in weighed], axis=0))
         return carry
 
     lax.fori_loop(0, (count + tile - 1) // tile, one_tile, 0)
@@ -214,20 +237,10 @@
         span = min(vocab, tokens * 16)
         for i in range(tokens * 16 // span):
             pltpu.make_async_copy(embedding.at[pl.ds(0, span)], blocks.at[pl.ds(i * span, span)], sem.at[0]).wait()
-        lane = lax.broadcasted_iota(jnp.int32, (16, 256), 1)
-        owner = lane // 16 == lax.broadcasted_iota(jnp.int32, (16, 256), 0)
-
-        def pick(i, carry):
-            rem = rem_ref[pl.ds(pl.multiple_of(i * 16, 16), 16), 0:1]
-            chosen = jnp.logical_and(owner, lax.rem(lane, 16) == rem).astype(F32).astype(BF16)
-            block = blocks[pl.ds(pl.multiple_of(i * 256, 256), 256), :]
-            e_ref[pl.ds(pl.multiple_of(i * 16, 16), 16), :] = jnp.dot(chosen, block, preferred_element_type=F32).astype(BF16)
-            return carry
-        lax.fori_loop(0, tokens // 16, pick, 0)
-
-
-def finish_kernel(n, heads_n, steps, kv, o_ref, lse_ref, s_ref, s_lse, e_ref, weight, out_ref,
-                  side_o, side_l, line_o, line_l, pass_o, pass_l, share, flat, att_all, w_buf, part, landed,
+
+
+def finish_kernel(n, heads_n, steps, kv, vocab_own, o_ref, lse_ref, s_ref, s_lse, tokens_ref, weight, blocks, out_ref,
+                  side_o, side_l, line_o, line_l, pass_o, pass_l, share, flat, att_all, w_buf, e_buf, block_buf, part, landed,
                   local_sem, so1, ro1, sl1, rl1, so2, ro2, sl2, rl2, gs1, gr1, gs2, gr2, hs, hr):
     rows, queries, width = s_ref.shape
     outer, inner = split_axis(n)
@@ -237,6 +250,8 @@
     a, b = me // inner, lax.rem(me, inner)
     load = pltpu.make_async_copy(weight, w_buf, local_sem.at[0])
     load.start()
+    fetch = pltpu.make_async_copy(blocks, block_buf, local_sem.at[1])
+    fetch.start()
     greet([{"seq": d} for d in line[1:] + side[1:]] + [{"head": lax.rem(head + i, heads_n)} for i in range(1, heads_n)])
     order = list(range(1, outer)) + [0]
 
@@ -274,7 +289,7 @@
             write(r, mixed)
             return carry
 
-        lax.fori_loop(0, rows, one_row, 0)
+        lax.fori_loop(0, rows, one_row, 0, unroll=4)
         return peak + jnp.log2(total)
 
     for k in order:
@@ -319,40 +334,74 @@
         att_all[me, :, h * width:(h + 1) * width] = flat[pl.ds(h, rows * steps, stride=heads), :].astype(BF16)
     gather = Gather(n, me, [att_all], gs1, gr1, gs2, gr2)
     gather.start()
+
+    vocab, (token_rows, _) = vocab_own, tokens_ref.shape
+    first_id = head * vocab
+    each = 16 // steps
+    lane = lax.broadcasted_iota(jnp.int32, (16, 256), 1)
+    owner = lane // 16 == lax.broadcasted_iota(jnp.int32, (16, 256), 0)
+    fetch.wait()
+
+    def pick(i, carry):
+        wanted = jnp.full((16, 256), -1, jnp.int32)
+        for x in range(16):
+            token = tokens_ref[i * each + x // steps, x % steps] - first_id
+            inside = jnp.logical_and(token >= 0, token < vocab)
+            wanted = jnp.where(lane // 16 == x, jnp.where(inside, lax.rem(token, 16), -1), wanted)
+        chosen = jnp.logical_and(owner, lax.rem(lane, 16) == wanted).astype(F32).astype(BF16)
+        block = block_buf[pl.ds(pl.multiple_of(i * 256, 256), 256), :]
+        e_buf[pl.ds(pl.multiple_of(i * 16, 16), 16), :] = jnp.dot(chosen, block, preferred_element_type=F32)
+        return carry
+
+    groups = token_rows * steps // 16
     for k in range(1, outer):
+        lax.fori_loop(groups * (k - 1) // outer, groups * k // outer, pick, 0)
         gather.forward(k)
+    lax.fori_loop(groups * (outer - 1) // outer, groups, pick, 0)
     load.wait()
+
+    columns = part.shape[2]
+    tile = min(256, columns)
+    chunk = rows * steps
+    span = n // heads_n
+
+    def project(j, cols):
+        where = lax.rem(b + j, inner)
+        lhs = jnp.concatenate([att_all[x * inner + where] for x in range(outer)], axis=0)
+        done = jnp.dot(lhs, w_buf[:, cols], preferred_element_type=F32)
+        for x in range(outer):
+            shard = x * inner + where
+            at = pl.ds(pl.multiple_of(shard * chunk, chunk), chunk)
+            part[shard, :, cols] = (done[x * chunk:(x + 1) * chunk] + e_buf[at, cols]).astype(BF16)
+
+    def head_copy(i, q, cols):
+        peer = lax.rem(head + i, heads_n)
+        return remote(part.at[pl.ds(peer * span, span), :, cols], landed.at[i, :, :, cols], hs.at[i, q], hr.at[i, q], head=peer)
+
+    cuts = [slice(x, x + tile) for x in range(0, columns, tile)]
+    for cols in cuts:
+        project(0, cols)
     gather.finish()
-
-    columns = part.shape[2]
-    tile = 256
-    total_rows = n * rows * steps
-
-    def project(i, carry):
-        cols = pl.ds(pl.multiple_of(i * tile, tile), tile)
-        lhs = att_all[...].reshape(total_rows, att_all.shape[2])
-        done = jnp.dot(lhs, w_buf[:, cols], preferred_element_type=F32) + e_ref[:, cols].astype(F32)
-        part[:, :, cols] = done.astype(BF16).reshape(heads_n, total_rows // heads_n, tile)
-        return carry
-
-    lax.fori_loop(0, columns // tile, project, 0)
-
-    def head_copy(i):
-        peer = lax.rem(head + i, heads_n)
-        return remote(part.at[peer], landed.at[i], hs.at[i], hr.at[i], head=peer)
-
-    for i in range(1, heads_n):
-        copy = head_copy(i)
-        copy.start()
-        sent.append(copy)
-    for i in range(1, heads_n):
-        head_copy(i).wait_recv()
-    total = part[head].astype(F32)
-    for i in range(1, heads_n):
-        total = total + landed[i].astype(F32)
-    out_ref[...] = total.astype(BF16)
+    for q, cols in enumerate(cuts):
+        for j in range(1, inner):
+            project(j, cols)
+        for i in range(1, heads_n):
+            copy = head_copy(i, q, cols)
+            copy.start()
+            sent.append(copy)
+    for q, cols in enumerate(cuts):
+        for i in range(1, heads_n):
+            head_copy(i, q, cols).wait_recv()
+        total = part[pl.ds(head * span, span), :, cols].astype(F32)
+        for i in range(1, heads_n):
+            total = total + landed[i, :, :, cols].astype(F32)
+        out_ref[:, cols] = total.astype(BF16).reshape(span * chunk, tile)
     for copy in sent:
         copy.wait_send()
+
+
+def smem():
+    return pl.BlockSpec(memory_space=pltpu.SMEM)
 
 
 def vmem():
@@ -373,14 +422,13 @@
     dma = pltpu.SemaphoreType.DMA
 
     q_own = queries.reshape(steps, rows, kv, group, width).transpose(1, 2, 0, 3, 4).reshape(rows, kv, per, width)
-    ids_own = jnp.broadcast_to(prompt_ids, (rows, 128))
     fresh = jnp.pad(new_kv.transpose(0, 2, 3, 1, 4), ((0, 0), (0, 0), (0, 0), (0, 16 - steps), (0, 0)))
     live = suf + 128
     q_all, ids_all, s_mixed, s_lse = pl.pallas_call(
         functools.partial(share_kernel, n, scale2, steps),
         out_shape=(sds((n, rows, kv, per, width), BF16), sds((n, rows, 128), jnp.int32),
                    sds((rows, kv * per, width), F32), sds((rows, 128), F32)),
-        in_specs=[pl.BlockSpec(memory_space=pltpu.SMEM), vmem(), vmem(), vmem(), pl.BlockSpec(memory_space=pl.ANY)],
+        in_specs=[smem(), smem(), vmem(), vmem(), pl.BlockSpec(memory_space=pl.ANY)],
         out_specs=(vmem(),) * 4,
         scratch_shapes=[
             pltpu.VMEM((2, rows, suf * kv, width), BF16), pltpu.VMEM((2, suf * kv, width), F32),
@@ -388,39 +436,35 @@
             *gather_sems(n, 2)],
         compiler_params=pltpu.CompilerParams(collective_id=0, has_side_effects=True, vmem_limit_bytes=VMEM_BYTES),
         name="share_queries",
-    )(suffix_lengths.astype(jnp.int32), q_own, ids_own, fresh, suffix_kv.reshape(2, rows, suf * kv, width))
+    )(suffix_lengths.astype(jnp.int32), prompt_ids.astype(jnp.int32), q_own, fresh, suffix_kv.reshape(2, rows, suf * kv, width))
 
     tokens = all_rows * steps
     vocab = embedding.shape[0]
-    local_ids = token_ids.reshape(tokens) - lax.axis_index("head") * vocab
-    inside = (local_ids >= 0) & (local_ids < vocab)
-    rem = jnp.broadcast_to(jnp.where(inside, local_ids % 16, -1)[:, None], (tokens, 128))
     tile = 4
     fixed = lambda *shape: pl.BlockSpec(shape, lambda p, *_: (0,) * len(shape))
     cut = pl.BlockSpec((1, positions * kv, width), lambda p, *_: (p, 0, 0))
-    o_all, lse_all, embedded = pl.pallas_call(
+    o_all, lse_all, blocks = pl.pallas_call(
         functools.partial(prompt_kernel, scale2, tile),
-        out_shape=(sds((all_rows, kv * per, width), BF16), sds((all_rows, 128), F32), sds((tokens, embedding.shape[1]), BF16)),
-        grid_spec=pltpu.PrefetchScalarGridSpec(
-            num_scalar_prefetch=2, grid=(prompts,),
-            in_specs=[fixed(all_rows, kv, per, width), cut, cut, fixed(tokens, 128), pl.BlockSpec(memory_space=pl.ANY)],
-            out_specs=(fixed(all_rows, kv * per, width), fixed(all_rows, 128), fixed(tokens, embedding.shape[1])),
-            scratch_shapes=[
-                pltpu.SMEM((all_rows + tile,), jnp.int32), pltpu.VMEM((2, positions * kv, width), F32),
-                pltpu.VMEM((kv, positions, width), BF16), pltpu.VMEM((kv, positions, width), BF16),
-                pltpu.VMEM((tokens * 16, embedding.shape[1]), BF16), dma((1,))]),
+        out_shape=(sds((all_rows, kv * per, width), BF16), sds((all_rows, 128), F32), sds((tokens * 16, embedding.shape[1]), BF16)),
+        grid=(prompts,),
+        in_specs=[smem(), smem(), fixed(all_rows, kv, per, width), cut, cut, pl.BlockSpec(memory_space=pl.ANY)],
+        out_specs=(fixed(all_rows, kv * per, width), fixed(all_rows, 128), pl.BlockSpec(memory_space=pl.ANY)),
+        scratch_shapes=[
+            pltpu.SMEM((prompts * (all_rows + tile),), jnp.int32), pltpu.SMEM((prompts,), jnp.int32),
+            pltpu.VMEM((2, positions * kv, width), F32),
+            pltpu.VMEM((kv, positions, width), BF16), pltpu.VMEM((kv, positions, width), BF16), dma((1,))],
         compiler_params=pltpu.CompilerParams(vmem_limit_bytes=VMEM_BYTES),
         name="prompt_attention",
-    )(ids_all[:, :, 0].reshape(all_rows), local_ids, q_all.reshape(all_rows, kv, per, width),
-      prompt_keys.reshape(prompts, positions * kv, width), prompt_values.reshape(prompts, positions * kv, width), rem, embedding)
+    )(token_ids, ids_all.reshape(all_rows, 128), q_all.reshape(all_rows, kv, per, width),
+      prompt_keys.reshape(prompts, positions * kv, width), prompt_values.reshape(prompts, positions * kv, width), embedding)
 
     columns = out_weight.shape[1]
     out_rows = tokens // heads_n
     pair = dma((outer, inner))
     out = pl.pallas_call(
-        functools.partial(finish_kernel, n, heads_n, steps, kv),
+        functools.partial(finish_kernel, n, heads_n, steps, kv, embedding.shape[0]),
         out_shape=sds((out_rows, columns), BF16),
-        in_specs=[vmem()] * 5 + [pl.BlockSpec(memory_space=pl.ANY)],
+        in_specs=[vmem()] * 4 + [smem()] + [pl.BlockSpec(memory_space=pl.ANY)] * 2,
         out_specs=vmem(),
         scratch_shapes=[
             pltpu.VMEM((outer, inner, rows, kv * per, width), BF16), pltpu.VMEM((outer, inner, rows, 128), F32),
@@ -428,12 +472,13 @@
             pltpu.VMEM((outer, rows, kv * per, width), BF16), pltpu.VMEM((outer, rows, 128), F32),
             pltpu.VMEM((max(inner, outer + 1), rows, 128), F32), pltpu.VMEM((rows * kv * per, width), F32),
             pltpu.VMEM((n, rows * steps, heads * width), BF16), pltpu.VMEM(out_weight.shape, BF16),
-            pltpu.VMEM((heads_n, out_rows, columns), BF16), pltpu.VMEM((heads_n, out_rows, columns), BF16),
-            dma((1,)), pair, pair, pair, pair, dma((outer,)), dma((outer,)), dma((outer,)), dma((outer,)),
-            *gather_sems(n, 1), dma((heads_n,)), dma((heads_n,))],
+            pltpu.VMEM((tokens, columns), F32), pltpu.VMEM(blocks.shape, BF16),
+            pltpu.VMEM((n, rows * steps, columns), BF16), pltpu.VMEM((heads_n, n // heads_n, rows * steps, columns), BF16),
+            dma((2,)), pair, pair, pair, pair, dma((outer,)), dma((outer,)), dma((outer,)), dma((outer,)),
+            *gather_sems(n, 1), dma((heads_n, 8)), dma((heads_n, 8))],
         compiler_params=pltpu.CompilerParams(collective_id=1, has_side_effects=True, vmem_limit_bytes=VMEM_BYTES),
         name="finish",
-    )(o_all.reshape(n, rows, kv * per, width), lse_all.reshape(n, rows, 128), s_mixed, s_lse, embedded, out_weight)
+    )(o_all.reshape(n, rows, kv * per, width), lse_all.reshape(n, rows, 128), s_mixed, s_lse, token_ids, out_weight, blocks)
     return out.reshape(all_rows // heads_n, steps, columns)
 
 

time: 128 us -> 337 us (2.63)
  the two profiles are of different devices: /device:TPU:17 before, /device:TPU:21 now
where the time goes in v2:
time: 337 us
  Pallas kernels  330 us (98%)
  local copies, waits for them, and re-layouts  6.49 us (2%)
    pallas_call x1, Pallas kernels, shards(): pl.pallas_call(functools.partial(prompt_kernel, scale2, tile), out_shape=...  258 us
    pallas_call x1, Pallas kernels, shards(): pl.pallas_call(functools.partial(finish_kernel, n, heads_n, steps, kv, em...  55.1 us
    pallas_call x1, Pallas kernels, shards(): pl.pallas_call(functools.partial(share_kernel, n, scale2, steps), out_sha...  16.9 us

profile of v2, /device:TPU:21, one launch (start us, length us, event | category | flops | bytes accessed | tf_op | source)
XLA Modules:
  0.0 336.7 jit_solution(1123965421612499564)
XLA Ops:
  0.0 0.0 copy-start
  0.0 1.4 copy.13.prompt_ids
  1.4 1.4 copy.14.tokens_ref
  2.7 0.8 copy.18
  3.5 0.7 pad.4.fresh
  4.2 0.0 copy-done
  4.2 0.7 copy_bitcast_fusion.q_own
  4.9 16.9 %share_queries.1 = (bf16[8,8,2,32,128]{4,3,2,1,0:T(8,128)(2,1)}, s32[8,8,128]{2,1,0:T(8,128)}, f32[8,64,128]{2,1,0:T(8,128)}, f32[8,128]{1,0:T(8,128)}) custom-call(s32[8]{0:T(128)} %lengths.1, s32[8,1]{1,0:T(8,128)} %copy.13.prompt_ids, bf16[8,2,32,128]{3,2,1,0:T(8,128)(2,1)} %copy_bitcast_fusion.q_own, bf16[2,8,2,16,128]{4,3,2,1,0:T(8,128)(2,1)} %pad.4.fresh, ...), custom_call_target="tpu_custom_call" | custom-call | tf_op jit(solution)/shard_map/share_queries/pallas_call | solution.py:427
  21.8 258.1 %prompt_attention.1 = (bf16[64,64,128]{2,1,0:T(8,128)(2,1)}, f32[64,128]{1,0:T(8,128)}, bf16[4096,1024]{1,0:T(8,128)(2,1)}) custom-call(s32[64,4]{1,0:T(8,128)} %copy.14.tokens_ref, s32[64,128]{1,0:T(8,128)} %bitcast.24, bf16[64,2,32,128]{3,2,1,0:T(8,128)(2,1)} %bitcast.21, bf16[8,2048,128]{2,1,0:T(8,128)(2,1)} %bitcast.18, bf16[8,2048,128]{2,1,0:T(8,128)(2,1)} %bitcast.19, ...), custom_call_target="tpu_custom_call" | custom-call | tf_op jit(solution)/shard_map/prompt_attention/pallas_call | solution.py:446
  279.9 55.1 %finish.1 = bf16[64,1024]{1,0:T(8,128)(2,1)} custom-call(bf16[8,8,64,128]{3,2,1,0:T(8,128)(2,1)} %bitcast.20, f32[8,8,128]{2,1,0:T(8,128)} %bitcast.23, f32[8,64,128]{2,1,0:T(8,128)} %get-tuple-element.16.s_ref, f32[8,128]{1,0:T(8,128)} %get-tuple-element.17.s_lse, s32[64,4]{1,0:T(8,128)} %copy.14.tokens_ref, bf16[2048,1024]{1,0:T(8,128)(2,1)} %weight.1, ...), custom_call_target="tpu_custom_call" | custom-call | tf_op jit(solution)/shard_map/finish/pallas_call | solution.py:464
  335.0 1.6 reshape.39
Async XLA Ops:
  0.0 4.2 %copy-start = (bf16[4,8,16,128]{3,2,1,0:T(8,128)(2,1)S(1)}, bf16[4,8,16,128]{3,2,1,0:T(8,128)(2,1)}, u32[]{:S(2)}) copy-start(bf16[4,8,16,128]{3,2,1,0:T(8,128)(2,1)} %param.10) | copy-start | bytes 393220

commit v3 on v2

--- a/solution.py
+++ b/solution.py
@@ -129,7 +129,7 @@
     sublane = lax.broadcasted_iota(jnp.int32, (rows, 128), 0)
     ids_own = jnp.zeros((rows, 128), jnp.int32)
     for r in range(rows):
-        ids_own = jnp.where(sublane == r, prompt_ids[r, 0], ids_own)
+        ids_own = jnp.where(sublane == r, prompt_ids[0, r], ids_own)
     ids_all[me] = ids_own
     gather = Gather(n, me, [q_all, ids_all], send1, recv1, send2, recv2)
     gather.start()
@@ -147,9 +147,11 @@
         stats = []
         for part, store in ((0, keys), (1, values)):
             wide[part] = raw[part, r].astype(F32)
+            late = [fresh[part, u, r].astype(F32) for u in range(steps)]
             for c in range(kv):
                 store[c, 0:suf] = wide[part, pl.ds(c, suf, stride=kv), :].astype(BF16)
-                store[c, suf:suf + fresh.shape[3]] = fresh[part, r, c]
+                rows16 = [x[c:c + 1] for x in late] + [jnp.zeros((16 - steps, width), F32)]
+                store[c, suf:suf + 16] = jnp.concatenate(rows16, axis=0).astype(BF16)
         seen = jnp.logical_or(old, new)
         scores = [lax.dot_general(q_own[r, c], keys[c], NT, preferred_element_type=F32) for c in range(kv)]
         weighed = [weigh(jnp.where(seen, x, -jnp.inf), scale2) for x in scores]
@@ -169,30 +171,29 @@
 
 
 def prompt_kernel(scale2, tile, tokens_ref, ids, q_ref, k_ref, v_ref, embedding, o_ref, lse_ref, blocks,
-                  order, counts, wide, keys, values, sem):
+                  order, counts, wide, keys, values, staged, sem):
     p = pl.program_id(0)
     prompts = counts.shape[0]
     rows, kv, queries, width = q_ref.shape
     positions = k_ref.shape[1] // kv
     vocab = embedding.shape[0]
-    token_rows, steps = tokens_ref.shape
+    steps, token_rows = tokens_ref.shape
     tokens = token_rows * steps
     room = rows + tile
 
     @pl.when(p == 0)
     def _():
-        first_id = lax.axis_index("head") * vocab
-
         def fetch(r, carry):
             for t in range(steps):
-                local = jnp.clip(tokens_ref[r, t] - first_id, 0, vocab - 1)
+                local = lax.rem(tokens_ref[t, r], vocab)
                 first = pl.multiple_of(local // 16 * 16, 16)
                 to = pl.multiple_of((r * steps + t) * 16, 16)
-                pltpu.make_async_copy(embedding.at[pl.ds(first, 16)], blocks.at[pl.ds(to, 16)], sem.at[0]).start()
+                pltpu.make_async_copy(embedding.at[pl.ds(first, 16)], staged.at[pl.ds(to, 16)], sem.at[0]).start()
             return carry
 
         for i in range(prompts):
             counts[i] = 0
+        values[:, :, width:] = jnp.ones((kv, positions, width), BF16)
 
         def place(r, carry):
             mine = ids[r, 0]
@@ -212,7 +213,7 @@
     for source, store, part in ((k_ref, keys, 0), (v_ref, values, 1)):
         wide[part] = source[0].astype(F32)
         for c in range(kv):
-            store[c] = wide[part, pl.ds(c, positions, stride=kv), :].astype(BF16)
+            store[c, :, 0:width] = wide[part, pl.ds(c, positions, stride=kv), :].astype(BF16)
 
     def one_tile(i, carry):
         picked = [order[base + i * tile + j] for j in range(tile)]
@@ -220,23 +221,32 @@
         for c in range(kv):
             query = jnp.concatenate([q_ref[r, c] for r in picked], axis=0)
             scores.append(lax.dot_general(query, keys[c], NT, preferred_element_type=F32))
-        weighed = [weigh(x, scale2) for x in scores]
-        for c, (weights, inverse, _) in enumerate(weighed):
-            mixed = (jnp.dot(weights, values[c], preferred_element_type=F32) * inverse).astype(BF16)
+        lses = []
+        for c, score in enumerate(scores):
+            peak = jnp.max(score, axis=-1, keepdims=True)
+            weights = jnp.exp2((score - peak) * scale2).astype(BF16)
+            both = jnp.dot(weights, values[c], preferred_element_type=F32)
+            lses.append(peak * scale2 + jnp.log2(both[:, width:]))
+            mixed = (both[:, :width] / both[:, width:]).astype(BF16)
             for j, r in enumerate(picked):
                 o_ref[r, c * queries:(c + 1) * queries] = mixed[j * queries:(j + 1) * queries]
         for j, r in enumerate(picked):
             span = slice(j * queries, (j + 1) * queries)
-            lse_ref[pl.ds(r, 1), :] = to_row(jnp.concatenate([w[2][span] for w in weighed], axis=0))
+            lse_ref[pl.ds(r, 1), :] = to_row(jnp.concatenate([x[span] for x in lses], axis=0))
         return carry
 
     lax.fori_loop(0, (count + tile - 1) // tile, one_tile, 0)
 
-    @pl.when(p == pl.num_programs(0) - 1)
+    @pl.when(p == pl.num_programs(0) // 2)
     def _():
         span = min(vocab, tokens * 16)
         for i in range(tokens * 16 // span):
-            pltpu.make_async_copy(embedding.at[pl.ds(0, span)], blocks.at[pl.ds(i * span, span)], sem.at[0]).wait()
+            pltpu.make_async_copy(embedding.at[pl.ds(0, span)], staged.at[pl.ds(i * span, span)], sem.at[0]).wait()
+        pltpu.make_async_copy(staged, blocks, sem.at[1]).start()
+
+    @pl.when(p == pl.num_programs(0) - 1)
+    def _():
+        pltpu.make_async_copy(staged, blocks, sem.at[1]).wait()
 
 
 def finish_kernel(n, heads_n, steps, kv, vocab_own, o_ref, lse_ref, s_ref, s_lse, tokens_ref, weight, blocks, out_ref,
@@ -335,7 +345,7 @@
     gather = Gather(n, me, [att_all], gs1, gr1, gs2, gr2)
     gather.start()
 
-    vocab, (token_rows, _) = vocab_own, tokens_ref.shape
+    vocab, (_, token_rows) = vocab_own, tokens_ref.shape
     first_id = head * vocab
     each = 16 // steps
     lane = lax.broadcasted_iota(jnp.int32, (16, 256), 1)
@@ -345,7 +355,7 @@
     def pick(i, carry):
         wanted = jnp.full((16, 256), -1, jnp.int32)
         for x in range(16):
-            token = tokens_ref[i * each + x // steps, x % steps] - first_id
+            token = tokens_ref[x % steps, i * each + x // steps] - first_id
             inside = jnp.logical_and(token >= 0, token < vocab)
             wanted = jnp.where(lane // 16 == x, jnp.where(inside, lax.rem(token, 16), -1), wanted)
         chosen = jnp.logical_and(owner, lax.rem(lane, 16) == wanted).astype(F32).astype(BF16)
@@ -395,7 +405,7 @@
         total = part[pl.ds(head * span, span), :, cols].astype(F32)
         for i in range(1, heads_n):
             total = total + landed[i, :, :, cols].astype(F32)
-        out_ref[:, cols] = total.astype(BF16).reshape(span * chunk, tile)
+        out_ref[:, :, cols] = total.astype(BF16).reshape(out_ref.shape[:2] + (tile,))
     for copy in sent:
         copy.wait_send()
 
@@ -422,7 +432,6 @@
     dma = pltpu.SemaphoreType.DMA
 
     q_own = queries.reshape(steps, rows, kv, group, width).transpose(1, 2, 0, 3, 4).reshape(rows, kv, per, width)
-    fresh = jnp.pad(new_kv.transpose(0, 2, 3, 1, 4), ((0, 0), (0, 0), (0, 0), (0, 16 - steps), (0, 0)))
     live = suf + 128
     q_all, ids_all, s_mixed, s_lse = pl.pallas_call(
         functools.partial(share_kernel, n, scale2, steps),
@@ -436,7 +445,7 @@
             *gather_sems(n, 2)],
         compiler_params=pltpu.CompilerParams(collective_id=0, has_side_effects=True, vmem_limit_bytes=VMEM_BYTES),
         name="share_queries",
-    )(suffix_lengths.astype(jnp.int32), prompt_ids.astype(jnp.int32), q_own, fresh, suffix_kv.reshape(2, rows, suf * kv, width))
+    )(suffix_lengths.astype(jnp.int32), prompt_ids.astype(jnp.int32).T, q_own, new_kv, suffix_kv.reshape(2, rows, suf * kv, width))
 
     tokens = all_rows * steps
     vocab = embedding.shape[0]
@@ -452,18 +461,18 @@
         scratch_shapes=[
             pltpu.SMEM((prompts * (all_rows + tile),), jnp.int32), pltpu.SMEM((prompts,), jnp.int32),
             pltpu.VMEM((2, positions * kv, width), F32),
-            pltpu.VMEM((kv, positions, width), BF16), pltpu.VMEM((kv, positions, width), BF16), dma((1,))],
+            pltpu.VMEM((kv, positions, width), BF16), pltpu.VMEM((kv, positions, 2 * width), BF16),
+            pltpu.VMEM((tokens * 16, embedding.shape[1]), BF16), dma((2,))],
         compiler_params=pltpu.CompilerParams(vmem_limit_bytes=VMEM_BYTES),
         name="prompt_attention",
-    )(token_ids, ids_all.reshape(all_rows, 128), q_all.reshape(all_rows, kv, per, width),
+    )(token_ids.T, ids_all.reshape(all_rows, 128), q_all.reshape(all_rows, kv, per, width),
       prompt_keys.reshape(prompts, positions * kv, width), prompt_values.reshape(prompts, positions * kv, width), embedding)
 
     columns = out_weight.shape[1]
-    out_rows = tokens // heads_n
     pair = dma((outer, inner))
     out = pl.pallas_call(
         functools.partial(finish_kernel, n, heads_n, steps, kv, embedding.shape[0]),
-        out_shape=sds((out_rows, columns), BF16),
+        out_shape=sds((all_rows // heads_n, steps, columns), BF16),
         in_specs=[vmem()] * 4 + [smem()] + [pl.BlockSpec(memory_space=pl.ANY)] * 2,
         out_specs=vmem(),
         scratch_shapes=[
@@ -478,8 +487,8 @@
             *gather_sems(n, 1), dma((heads_n, 8)), dma((heads_n, 8))],
         compiler_params=pltpu.CompilerParams(collective_id=1, has_side_effects=True, vmem_limit_bytes=VMEM_BYTES),
         name="finish",
-    )(o_all.reshape(n, rows, kv * per, width), lse_all.reshape(n, rows, 128), s_mixed, s_lse, token_ids, out_weight, blocks)
-    return out.reshape(all_rows // heads_n, steps, columns)
+    )(o_all.reshape(n, rows, kv * per, width), lse_all.reshape(n, rows, 128), s_mixed, s_lse, token_ids.T, out_weight, blocks)
+    return out
 
 
 def solution(mesh):

time: 337 us -> 97.4 us (0.29)
  Pallas kernels: 330 us -> 94.2 us
    pallas_call x1, Pallas kernels: 258 us -> 22.4 us  [shards(): pl.pallas_call(functools.partial(prompt_kernel, scale2, tile), out_shape=...]
where the time goes in v3:
time: 97.4 us
  Pallas kernels  94.2 us (97%)
  local copies, waits for them, and re-layouts  3.19 us (3%)
    pallas_call x1, Pallas kernels, shards(): pl.pallas_call(functools.partial(finish_kernel, n, heads_n, steps, kv, em...  55.1 us
    pallas_call x1, Pallas kernels, shards(): pl.pallas_call(functools.partial(prompt_kernel, scale2, tile), out_shape=...  22.4 us
    pallas_call x1, Pallas kernels, shards(): pl.pallas_call(functools.partial(share_kernel, n, scale2, steps), out_sha...  16.7 us
    unnamed x3, local copies, waits for them, and re-layouts  2.51 us

profile of v3, /device:TPU:21, one launch (start us, length us, event | category | flops | bytes accessed | tf_op | source)
XLA Modules:
  0.0 97.4 jit_solution(2645332015343425258)
XLA Ops:
  0.0 0.0 copy-start
  0.0 0.9 copy-done
  0.9 0.7 copy_bitcast_fusion.q_own
  1.6 16.7 %share_queries.1 = (bf16[8,8,2,32,128]{4,3,2,1,0:T(8,128)(2,1)}, s32[8,8,128]{2,1,0:T(8,128)}, f32[8,64,128]{2,1,0:T(8,128)}, f32[8,128]{1,0:T(8,128)}) custom-call(s32[8]{0:T(128)} %lengths.1, s32[1,8]{1,0:T(1,128)} %bitcast.25, bf16[8,2,32,128]{3,2,1,0:T(8,128)(2,1)} %copy_bitcast_fusion.q_own, bf16[2,4,8,2,128]{4,3,2,1,0:T(2,128)(2,1)} %fresh.1, ...), custom_call_target="tpu_custom_call" | custom-call | tf_op jit(solution)/shard_map/share_queries/pallas_call | solution.py:436
  18.3 22.4 %prompt_attention.1 = (bf16[64,64,128]{2,1,0:T(8,128)(2,1)}, f32[64,128]{1,0:T(8,128)}, bf16[4096,1024]{1,0:T(8,128)(2,1)}) custom-call(s32[4,64]{1,0:T(4,128)} %bitcast.23, s32[64,128]{1,0:T(8,128)} %bitcast.21, bf16[64,2,32,128]{3,2,1,0:T(8,128)(2,1)} %bitcast.19, bf16[8,2048,128]{2,1,0:T(8,128)(2,1)} %bitcast.16, bf16[8,2048,128]{2,1,0:T(8,128)(2,1)} %bitcast.17, ...), custom_call_target="tpu_custom_call" | custom-call | tf_op jit(solution)/shard_map/prompt_attention/pallas_call | solution.py:455
  40.7 55.1 %finish.1 = bf16[16,4,1024]{2,1,0:T(4,128)(2,1)} custom-call(bf16[8,8,64,128]{3,2,1,0:T(8,128)(2,1)} %bitcast.20, f32[8,8,128]{2,1,0:T(8,128)} %bitcast.22, f32[8,64,128]{2,1,0:T(8,128)} %get-tuple-element.16.s_ref, f32[8,128]{1,0:T(8,128)} %get-tuple-element.17.s_lse, s32[4,64]{1,0:T(4,128)} %bitcast.24, bf16[2048,1024]{1,0:T(8,128)(2,1)} %weight.1, ...), custom_call_target="tpu_custom_call" | custom-call | tf_op jit(solution)/shard_map/finish/pallas_call | solution.py:473
  95.8 1.6 %copy.14 = bf16[16,4,1024]{2,1,0:T(4,128)(2,1)} copy(bf16[16,4,1024]{2,1,0:T(4,128)(2,1)} %finish.1) | data formatting | bytes 262144
Async XLA Ops:
  0.0 0.9 copy-start
